TPU v7x, 256 devices: a whole 4x4x8 slice. The times are simulated.
256 devices in a mesh: kc: 8 (over x, y_lo), kb: 16 (over z, core), occ: 2 (over y_hi).
Axes of the slice: x: 4, y: 4 (y_hi: 2, y_lo: 2; y = y_hi * 2 + y_lo), z: 8, core: 2. Of those that a mesh axis runs over, the one named last changes fastest.
Arguments:
- amplitudes: bfloat16 [16, 2, 64, 1024], P('kb'), may hold values from -6 to 6
- integrals: bfloat16 [16, 2, 32, 8, 1024], P('kb', None, None, 'occ'), may hold values from -0.109375 to 0.109375
- eps_occ: float32 [8], replicated, as said below
- eps_vir: float32 [16, 32], replicated, as said below
- conserve: int32 [16, 16], replicated, may hold values from 0 to 15, as said below
- partner: int32 [16], replicated, may hold values from 0 to 15, as said below
Outputs:
- lambda_source: float32 [16, 2, 64, 1024], P('kb', None, ('kc', 'occ'))
Inputs may be any that keep to these rules, and one draw needn't show every extreme that they name: conserve[kb, kc] is the label of ka + kb - kc on the periodic 4 x 4 k-mesh for one fixed ka; for every kc it is a permutation over kb, and for every kb a permutation over kc. partner[k] is the label of -k on the same k-mesh; partner of partner is k itself. `eps_occ`: every occupied energy is a whole multiple of 1/32 from -1 to 1. `eps_vir`: every virtual energy is a whole multiple of 1/32 from -1 to 2.
All inputs are finite; a program needn't handle non-finite values.
Results may differ from a plain program's by a relative error of at most 0.0031.
Values may be sent and summed in bfloat16 or wider, within the bound.
A program may use at most 256 MiB of HBM per device.

v0:
```python
import functools

import jax
import jax.numpy as jnp
from jax import lax
from jax.experimental import pallas as pl
from jax.experimental.pallas import tpu as pltpu
from jax.sharding import PartitionSpec as P

KC = 8
KB = 16
OCC = 2
POS = KC * OCC
LANES = 128
PAIRS = 64
GROUPS = 8
HALF = 32
ROWS = GROUPS * HALF
DEPTH = 32
TILES = 32
CHUNK = 16
SHIFT = 2.0**-18
MESH = pl.DeviceIdType.MESH
F32 = jnp.float32
BF16 = jnp.bfloat16


def place(position, kb):
    return {"kc": position // OCC, "kb": kb, "occ": position % OCC}


def kernel(
    conserve, partner, eps_occ, eps_vir, amp, slab, out,
    abuf, symbuf, lhs, ztop, zbot, row_den, col_den, acc, o1_send, o1_recv0, o1_recv1, o2_send, o2_recv,
    beta, holder, copy_sem, h1_send, h1_recv, h2_send, h2_recv, p1_send, p1_recv, p2_send, p2_recv,
):
    kc = lax.axis_index("kc")
    kb = lax.axis_index("kb")
    occ = lax.axis_index("occ")
    pos = kc * OCC + occ
    core = kb % 2
    plane = kb - core
    spot = pos * 2 + core
    part = pos // GROUPS
    group = pos % GROUPS

    o1_recv = (o1_recv0, o1_recv1)
    barrier = pltpu.get_barrier_semaphore()

    @pl.loop(1, KB)
    def _(step):
        pl.semaphore_signal(
            barrier, inc=1, device_id=place(pos, (kb + step) % KB), device_id_type=MESH
        )

    @pl.loop(1, POS)
    def _(step):
        for other in range(2):
            pl.semaphore_signal(
                barrier,
                inc=1,
                device_id=place((pos + step) % POS, plane + other),
                device_id_type=MESH,
            )

    own = pltpu.make_async_copy(
        amp.at[0, part, :, pl.ds(pl.multiple_of(group * LANES, LANES), LANES)],
        abuf.at[kb],
        copy_sem,
    )
    own.start()
    own.wait()
    pl.semaphore_wait(barrier, KB - 1 + 2 * (POS - 1))

    @pl.loop(1, KB)
    def _(step):
        pltpu.make_async_remote_copy(
            src_ref=abuf.at[kb],
            dst_ref=abuf.at[kb],
            send_sem=h1_send,
            recv_sem=h1_recv,
            device_id=place(pos, (kb + step) % KB),
            device_id_type=MESH,
        ).start()

    ztop[...] = jnp.zeros_like(ztop)
    zbot[...] = jnp.zeros_like(zbot)
    for k in range(4):
        real = slab[0, 0, :, k, :]
        imag = slab[0, 1, :, k, :]
        for u in range(8):
            at = (k * 8 + u) * 2 * LANES
            re = real[:, u * LANES : (u + 1) * LANES]
            im = imag[:, u * LANES : (u + 1) * LANES]
            ztop[3 * DEPTH : 4 * DEPTH, at : at + LANES] = re
            ztop[3 * DEPTH : 4 * DEPTH, at + LANES : at + 2 * LANES] = im
            zbot[3 * DEPTH : 4 * DEPTH, at : at + LANES] = -im
            zbot[3 * DEPTH : 4 * DEPTH, at + LANES : at + 2 * LANES] = re

    for p in range(KC):
        found = jnp.int32(0)
        for label in range(KB):
            found = found + jnp.where(conserve[label, p] == kb, label, 0)
        beta[p] = jnp.minimum(found, KB - 1)
    for c in range(2):
        for label in range(KB):
            left = jnp.int32(KC)
            for p in range(KC):
                left = left - jnp.where(conserve[label, p] == plane + c, KC - p, 0)
            holder[c * KB + label] = jnp.maximum(left, 0)
    mine = jnp.int32(0)
    for label in range(KB):
        mine = mine + jnp.where(conserve[label, kc] == kb, label, 0)
    mine = jnp.minimum(mine, KB - 1)

    row = lax.broadcasted_iota(jnp.int32, (HALF, LANES), 0)
    lane = lax.broadcasted_iota(jnp.int32, (8, LANES), 1)
    for h in range(2):
        i_of = row // 4
        j_of = (row // 2) % 2 * 4 + h * 2 + row % 2
        pair = jnp.full((HALF, LANES), -SHIFT, F32)
        for k in range(8):
            pair = pair + jnp.where(i_of == k, eps_occ[k], 0.0)
            pair = pair + jnp.where(j_of == k, eps_occ[k], 0.0)
        for a in range(DEPTH):
            g, sub = a // 4, a % 4
            row_den[h, sub, g * HALF : (g + 1) * HALF, :] = pair - eps_vir[mine, a]
    vir_c = jnp.zeros((8, LANES), F32)
    for c in range(DEPTH):
        vir_c = vir_c + jnp.where(lane % DEPTH == c, eps_vir[kb, c], 0.0)
    for u in range(8):
        vir_bc = vir_c
        for s in range(4):
            vir_bc = vir_bc + jnp.where(lane // DEPTH == s, eps_vir[kc, u * 4 + s], 0.0)
        for k in range(4):
            col_den[k * 8 + u] = eps_occ[occ * 4 + k] - vir_bc

    for zero in range(4):
        o1_recv0[2 * POS + zero] = jnp.zeros((16, LANES), BF16)
        o1_recv1[2 * POS + zero] = jnp.zeros((16, LANES), BF16)

    out_row = lax.broadcasted_iota(jnp.int32, (PAIRS, 2 * PAIRS), 0)
    in_col = lax.broadcasted_iota(jnp.int32, (PAIRS, 2 * PAIRS), 1)
    h_of = out_row // HALF
    i_of = out_row % HALF // 4
    j_of = out_row % HALF // 2 % 2 * 4 + h_of * 2 + out_row % 2
    sign = (1 - 2 * part).astype(F32)
    order = jnp.where(in_col == i_of * 8 + j_of, 1.0, 0.0) + jnp.where(
        in_col == PAIRS + j_of * 8 + i_of, sign, 0.0
    )
    order = order.astype(BF16)

    whole = pltpu.make_async_remote_copy(
        src_ref=abuf.at[pl.ds(0, KB - 1)],
        dst_ref=abuf.at[pl.ds(0, KB - 1)],
        send_sem=h1_send,
        recv_sem=h1_recv,
        device_id=place(pos, (kb + 1) % KB),
        device_id_type=MESH,
    )
    whole.wait_recv()
    for p in range(KC):
        label = beta[p]
        both = jnp.concatenate([abuf[label], abuf[partner[label]]], axis=0)
        sym = jnp.dot(order, both, preferred_element_type=F32).astype(BF16)
        symbuf[0, p] = sym[:HALF]
        symbuf[1, p] = sym[HALF:]
    for h in range(2):
        lhs[h, pos] = symbuf[h, kc]

        @pl.loop(1, POS)
        def _(step):
            to = (pos + step) % POS
            pltpu.make_async_remote_copy(
                src_ref=symbuf.at[h, to // OCC],
                dst_ref=lhs.at[h, pos],
                send_sem=h2_send.at[h],
                recv_sem=h2_recv.at[h],
                device_id=place(to, kb),
                device_id_type=MESH,
            ).start()

    perm_row = lax.broadcasted_iota(jnp.int32, (ROWS, ROWS), 0)
    perm_col = lax.broadcasted_iota(jnp.int32, (ROWS, ROWS), 1)
    perm_from = perm_row % 16 // 2 * HALF + perm_row // 16 * 2 + perm_row % 2
    perm = jnp.where(perm_col == perm_from, 1.0, 0.0).astype(BF16)

    def lhs_wait(h):
        return pltpu.make_async_remote_copy(
            src_ref=lhs.at[h, pl.ds(0, POS - 1)],
            dst_ref=lhs.at[h, pl.ds(0, POS - 1)],
            send_sem=h2_send.at[h],
            recv_sem=h2_recv.at[h],
            device_id=place((pos + 1) % POS, kb),
            device_id_type=MESH,
        )

    def multiply(h, first, last):
        left = jnp.concatenate(
            [
                lhs[h, 0:GROUPS].reshape(ROWS, LANES),
                lhs[h, GROUPS:POS].reshape(ROWS, LANES),
            ],
            axis=1,
        )

        @pl.loop(first, last)
        def _(step):
            sub = step // (TILES // CHUNK)
            chunk = step % (TILES // CHUNK)
            at = pl.multiple_of(chunk * (CHUNK * 2 * LANES), CHUNK * 2 * LANES)
            down = pl.multiple_of((3 - sub) * DEPTH, DEPTH)
            weight = jnp.concatenate(
                [
                    ztop[pl.ds(down, 4 * DEPTH), pl.ds(at, CHUNK * 2 * LANES)],
                    zbot[pl.ds(down, 4 * DEPTH), pl.ds(at, CHUNK * 2 * LANES)],
                ],
                axis=0,
            )
            product = jnp.dot(left, weight, preferred_element_type=F32)
            den_row = row_den[h, sub]
            parts = []
            for s in range(CHUNK):
                den = den_row + col_den[chunk * CHUNK + s, 0:1, :]
                inverse = jnp.clip(pltpu.reciprocal(den, approx=True), -1.0, 1.0)
                lo = s * 2 * LANES
                parts.append((product[:, lo : lo + LANES] * inverse).astype(BF16))
                parts.append((product[:, lo + LANES : lo + 2 * LANES] * inverse).astype(BF16))
            scaled = jnp.concatenate(parts, axis=1)
            acc[...] += lax.dot_general(
                scaled, weight, (((1,), (1,)), ((), ())), preferred_element_type=F32
            )

    def send_partials(h):
        packed = jnp.dot(perm, acc[...].astype(BF16), preferred_element_type=F32).astype(BF16)
        for r in range(POS):
            for c in range(2):
                o1_send[h, r * 2 + c] = packed[r * 16 : (r + 1) * 16, c * LANES : (c + 1) * LANES]
        o1_recv[h][spot] = o1_send[h, spot]

        @pl.loop(1, 2 * POS)
        def _(step):
            to = (spot + step) % (2 * POS)
            pltpu.make_async_remote_copy(
                src_ref=o1_send.at[h, to],
                dst_ref=o1_recv[h].at[spot],
                send_sem=p1_send.at[h],
                recv_sem=p1_recv.at[h],
                device_id=place(to // 2, plane + to % 2),
                device_id_type=MESH,
            ).start()

    def partials_wait(h):
        return pltpu.make_async_remote_copy(
            src_ref=o1_send.at[h, pl.ds(0, 2 * POS - 1)],
            dst_ref=o1_recv[h].at[pl.ds(0, 2 * POS - 1)],
            send_sem=p1_send.at[h],
            recv_sem=p1_recv.at[h],
            device_id=place((pos + 1) % POS, kb),
            device_id_type=MESH,
        )

    def send_sums(h):
        partials_wait(h).wait_recv()

        for label in range(KB):
            total = jnp.zeros((16, LANES), F32)
            for c in range(2):
                p = holder[c * KB + label]
                for o in range(OCC):
                    total = total + o1_recv[h][(p * OCC + o) * 2 + c].astype(F32)
            o2_send[h, label] = total.astype(BF16)
        o2_recv[h, kb] = o2_send[h, kb]

        @pl.loop(1, KB)
        def _(step):
            to = (kb + step) % KB
            pltpu.make_async_remote_copy(
                src_ref=o2_send.at[h, to],
                dst_ref=o2_recv.at[h, kb],
                send_sem=p2_send.at[h],
                recv_sem=p2_recv.at[h],
                device_id=place(pos, to),
                device_id_type=MESH,
            ).start()

    def sums_wait(h):
        return pltpu.make_async_remote_copy(
            src_ref=o2_send.at[h, pl.ds(0, KB - 1)],
            dst_ref=o2_recv.at[h, pl.ds(0, KB - 1)],
            send_sem=p2_send.at[h],
            recv_sem=p2_recv.at[h],
            device_id=place(pos, (kb + 1) % KB),
            device_id_type=MESH,
        )

    def finish(h):
        sums_wait(h).wait_recv()
        for c in range(2):
            total = jnp.zeros((16, LANES), F32)
            for z in range(KB // 2):
                total = total + o2_recv[h, z * 2 + c].astype(F32)
            out[h, c] = total

    steps = 4 * TILES // CHUNK
    lhs_wait(0).wait_recv()
    acc[...] = jnp.zeros_like(acc)
    multiply(0, 0, steps)
    send_partials(0)
    lhs_wait(1).wait_recv()
    acc[...] = jnp.zeros_like(acc)
    multiply(1, 0, steps // 2)
    send_sums(0)
    multiply(1, steps // 2, steps)
    send_partials(1)
    finish(0)
    send_sums(1)
    whole.wait_send()
    for h in range(2):
        lhs_wait(h).wait_send()
        partials_wait(h).wait_send()
    finish(1)
    for h in range(2):
        sums_wait(h).wait_send()


def shards(amplitudes, integrals, eps_occ, eps_vir, conserve, partner):
    smem = pl.BlockSpec(memory_space=pltpu.SMEM)
    vmem = pl.BlockSpec(memory_space=pltpu.VMEM)
    result = pl.pallas_call(
        kernel,
        out_shape=jax.ShapeDtypeStruct((2, 2, 16, LANES), F32),
        in_specs=[smem, smem, smem, smem, pl.BlockSpec(memory_space=pl.ANY), vmem],
        out_specs=vmem,
        scratch_shapes=[
            pltpu.VMEM((KB, PAIRS, LANES), BF16),
            pltpu.VMEM((2, KC, HALF, LANES), BF16),
            pltpu.VMEM((2, POS, HALF, LANES), BF16),
            pltpu.VMEM((7 * DEPTH, TILES * 2 * LANES), BF16),
            pltpu.VMEM((7 * DEPTH, TILES * 2 * LANES), BF16),
            pltpu.VMEM((2, 4, ROWS, LANES), F32),
            pltpu.VMEM((TILES, 8, LANES), F32),
            pltpu.VMEM((ROWS, 2 * LANES), F32),
            pltpu.VMEM((2, 2 * POS, 16, LANES), BF16),
            pltpu.VMEM((2 * POS + 4, 16, LANES), BF16),
            pltpu.VMEM((2 * POS + 4, 16, LANES), BF16),
            pltpu.VMEM((2, KB, 16, LANES), BF16),
            pltpu.VMEM((2, KB, 16, LANES), BF16),
            pltpu.SMEM((KC,), jnp.int32),
            pltpu.SMEM((2 * KB,), jnp.int32),
            pltpu.SemaphoreType.DMA,
            pltpu.SemaphoreType.DMA,
            pltpu.SemaphoreType.DMA,
        ]
        + [pltpu.SemaphoreType.DMA((2,))] * 6,
        compiler_params=pltpu.CompilerParams(
            collective_id=0, has_side_effects=True, vmem_limit_bytes=60 * 2**20
        ),
        name="lambda_source",
    )(conserve, partner, eps_occ, eps_vir, amplitudes, integrals)
    result = result.reshape(2, 2, GROUPS, 2, LANES)
    return jnp.transpose(result, (1, 0, 3, 2, 4)).reshape(1, 2, 4, GROUPS * LANES)


def solution(mesh):
    in_specs = (P("kb", None, None, None), P("kb", None, None, "occ", None), P(), P(), P(), P())
    out_specs = P("kb", None, ("kc", "occ"), None)
    return jax.shard_map(shards, mesh=mesh, in_specs=in_specs, out_specs=out_specs, check_vma=False)
```

profile of v0, /device:TPU:1, one launch (start us, length us, event | category | flops | bytes accessed | tf_op | source)
XLA Modules:
  0.0 62.0 jit_solution(3968797297637136451)
XLA Ops:
  0.0 60.6 %lambda_source.1 = f32[2,2,16,128]{3,2,1,0:T(8,128)} custom-call(s32[16,16]{1,0:T(8,128)} %conserve.1, s32[16]{0:T(128)} %partner.1, f32[8]{0:T(128)} %eps_occ.1, f32[16,32]{1,0:T(8,128)} %eps_vir.1, bf16[1,2,64,1024]{3,2,1,0:T(8,128)(2,1)} %amp.1, bf16[1,2,32,4,1024]{4,3,2,1,0:T(4,128)(2,1)} %slab.1), custom_call_target="tpu_custom_call" | custom-call | tf_op jit(solution)/shard_map/lambda_source/pallas_call | solution.py:330
  60.6 0.8 %copy.7 = f32[2,2,2,8,128]{4,3,2,1,0:T(8,128)S(1)} copy(f32[2,2,2,8,128]{4,2,3,0,1:T(2,128)} %bitcast.5) | data formatting | bytes 65536 | tf_op jit(solution)/shard_map/transpose | solution.py:362
  61.4 0.6 %reshape.7 = f32[1,2,4,1024]{3,2,1,0:T(4,128)} reshape(f32[2,2,2,8,128]{4,3,2,1,0:T(8,128)S(1)} %copy.7) | data formatting | bytes 65536 | tf_op jit(solution)/shard_map/reshape | solution.py:362
where the time goes:
time: 62.2 us; the launch traced here: 62 us
  Pallas kernels  60.6 us (97%)
  local copies, waits for them, and re-layouts  1.39 us (2%)
    pallas_call x1, Pallas kernels, shards(): pl.pallas_call(kernel, out_shape=jax.ShapeDtypeStruct((2, 2, 16, LANES),...  60.6 us

commit v1 on v0

v1 whole, which is shorter than its diff:
```python
import functools

import jax
import jax.numpy as jnp
from jax import lax
from jax.experimental import pallas as pl
from jax.experimental.pallas import tpu as pltpu
from jax.sharding import PartitionSpec as P

KC = 8
KB = 16
OCC = 2
POS = KC * OCC
LANES = 128
PAIRS = 64
GROUPS = 8
HALF = 32
ROWS = GROUPS * HALF
DEPTH = 32
TILES = 32
CHUNK = 32
SHIFT = 2.0**-18
DEEP = 8
ORDER = (1, 7, 2, 6, 3, 5, 4)
MESH = pl.DeviceIdType.MESH
F32 = jnp.float32
BF16 = jnp.bfloat16


def place(position, kb):
    return {"kc": position // OCC, "kb": kb, "occ": position % OCC}


def kernel(
    conserve_in, partner_in, eps_occ_in, eps_vir_in, amp, slab_in, out,
    conserve, partner, eps_occ, eps_vir, slab, load_sem, abuf, symbuf, lhs, ztop, zbot, row_den, col_den, acc, o1_send, o1_recv0, o1_recv1,
    sums, sums_recv, o2_send, o2_recv, last_send, last_recv, beta, holder, ready, copy_sem, h1_send, h1_recv, fwd_send, fwd_recv,
    h2_send, h2_recv, p1_send, p1_recv, sib_send, sib_recv, p2_send, p2_recv, last_sems,
):
    kc = lax.axis_index("kc")
    kb = lax.axis_index("kb")
    occ = lax.axis_index("occ")
    pos = kc * OCC + occ
    core = kb % 2
    z = kb // 2
    sibling = {"kb": kb + 1 - 2 * core}
    part = pos // GROUPS
    group = pos % GROUPS
    x = kc // 2
    y_lo = kc % 2
    y = occ * 2 + y_lo

    def along_z(step):
        return {"kb": (z + step) % DEEP * 2 + core}

    def along_y(step):
        to = (y + step) % 4
        return {"kc": x * 2 + to % 2, "occ": to // 2}

    o1_recv = (o1_recv0, o1_recv1)
    barrier = pltpu.get_barrier_semaphore()

    for step in ORDER:
        pl.semaphore_signal(barrier, inc=1, device_id=along_z(step), device_id_type=MESH)
    pl.semaphore_signal(barrier, inc=1, device_id=sibling, device_id_type=MESH)
    for step in range(1, 4):
        pl.semaphore_signal(
            barrier,
            inc=1,
            device_id={"kc": (x + step) % 4 * 2 + y_lo},
            device_id_type=MESH,
        )
        pl.semaphore_signal(barrier, inc=1, device_id=along_y(step), device_id_type=MESH)

    own = pltpu.make_async_copy(
        amp.at[0, part, :, pl.ds(pl.multiple_of(group * LANES, LANES), LANES)],
        abuf.at[kb],
        copy_sem,
    )
    own.start()
    loads = [
        pltpu.make_async_copy(source, target, load_sem.at[at])
        for at, (source, target) in enumerate(
            (
                (slab_in, slab),
                (conserve_in, conserve),
                (partner_in, partner),
                (eps_occ_in, eps_occ),
                (eps_vir_in, eps_vir),
            )
        )
    ]
    for load in loads:
        load.start()
    own.wait()
    pl.semaphore_wait(barrier, DEEP + 6)

    def stripe_copy(step):
        return pltpu.make_async_remote_copy(
            src_ref=abuf.at[kb],
            dst_ref=abuf.at[kb],
            send_sem=h1_send,
            recv_sem=h1_recv.at[z],
            device_id=along_z(step),
            device_id_type=MESH,
        )

    def forward(label):
        pltpu.make_async_remote_copy(
            src_ref=abuf.at[label],
            dst_ref=abuf.at[label],
            send_sem=fwd_send,
            recv_sem=fwd_recv,
            device_id=sibling,
            device_id_type=MESH,
        ).start()

    for step in ORDER:
        stripe_copy(step).start()
    for step in range(1, 4):
        pl.semaphore_signal(ready, inc=1, device_id=along_y(step), device_id_type=MESH)
    forward(kb)

    ztop[...] = jnp.zeros_like(ztop)
    zbot[...] = jnp.zeros_like(zbot)
    for load in loads:
        load.wait()
    for k in range(4):
        real = slab[0, 0, :, k, :]
        imag = slab[0, 1, :, k, :]
        for u in range(8):
            at = (k * 8 + u) * 2 * LANES
            re = real[:, u * LANES : (u + 1) * LANES]
            im = imag[:, u * LANES : (u + 1) * LANES]
            ztop[3 * DEPTH : 4 * DEPTH, at : at + LANES] = re
            ztop[3 * DEPTH : 4 * DEPTH, at + LANES : at + 2 * LANES] = im
            zbot[3 * DEPTH : 4 * DEPTH, at : at + LANES] = -im
            zbot[3 * DEPTH : 4 * DEPTH, at + LANES : at + 2 * LANES] = re

    for p in range(KC):
        found = jnp.int32(0)
        for label in range(KB):
            found = found + jnp.where(conserve[label, p] == kb, label, 0)
        beta[p] = jnp.minimum(found, KB - 1)
    for label in range(KB):
        left = jnp.int32(KC)
        for p in range(KC):
            left = left - jnp.where(conserve[label, p] == kb, KC - p, 0)
        holder[label] = jnp.maximum(left, 0)
    mine = jnp.int32(0)
    for label in range(KB):
        mine = mine + jnp.where(conserve[label, kc] == kb, label, 0)
    mine = jnp.minimum(mine, KB - 1)

    row = lax.broadcasted_iota(jnp.int32, (HALF, LANES), 0)
    lane = lax.broadcasted_iota(jnp.int32, (8, LANES), 1)
    for h in range(2):
        i_of = row // 4
        j_of = (row // 2) % 2 * 4 + h * 2 + row % 2
        pair = jnp.full((HALF, LANES), -SHIFT, F32)
        for k in range(8):
            pair = pair + jnp.where(i_of == k, eps_occ[k], 0.0)
            pair = pair + jnp.where(j_of == k, eps_occ[k], 0.0)
        for a in range(DEPTH):
            g, sub = a // 4, a % 4
            row_den[h, sub, g * HALF : (g + 1) * HALF, :] = pair - eps_vir[mine, a]
    vir_c = jnp.zeros((8, LANES), F32)
    for c in range(DEPTH):
        vir_c = vir_c + jnp.where(lane % DEPTH == c, eps_vir[kb, c], 0.0)
    for u in range(8):
        vir_bc = vir_c
        for s in range(4):
            vir_bc = vir_bc + jnp.where(lane // DEPTH == s, eps_vir[kc, u * 4 + s], 0.0)
        for k in range(4):
            col_den[k * 8 + u] = eps_occ[occ * 4 + k] - vir_bc

    for zero in range(OCC):
        o1_recv0[POS + zero] = jnp.zeros((16, 2 * LANES), BF16)
        o1_recv1[POS + zero] = jnp.zeros((16, 2 * LANES), BF16)

    out_row = lax.broadcasted_iota(jnp.int32, (PAIRS, 2 * PAIRS), 0)
    in_col = lax.broadcasted_iota(jnp.int32, (PAIRS, 2 * PAIRS), 1)
    h_of = out_row // HALF
    i_of = out_row % HALF // 4
    j_of = out_row % HALF // 2 % 2 * 4 + h_of * 2 + out_row % 2
    sign = (1 - 2 * part).astype(F32)
    order = jnp.where(in_col == i_of * 8 + j_of, 1.0, 0.0) + jnp.where(
        in_col == PAIRS + j_of * 8 + i_of, sign, 0.0
    )
    order = order.astype(BF16)

    perm_row = lax.broadcasted_iota(jnp.int32, (ROWS, ROWS), 0)
    perm_col = lax.broadcasted_iota(jnp.int32, (ROWS, ROWS), 1)
    perm_from = perm_row % 16 // 2 * HALF + perm_row // 16 * 2 + perm_row % 2
    perm = jnp.where(perm_col == perm_from, 1.0, 0.0).astype(BF16)

    for step in ORDER:
        came = (z + DEEP - step) % DEEP
        pltpu.make_async_remote_copy(
            src_ref=abuf.at[kb],
            dst_ref=abuf.at[kb],
            send_sem=h1_send,
            recv_sem=h1_recv.at[came],
            device_id=sibling,
            device_id_type=MESH,
        ).wait_recv()
        forward(came * 2 + core)
    forwarded = pltpu.make_async_remote_copy(
        src_ref=abuf.at[pl.ds(0, DEEP)],
        dst_ref=abuf.at[pl.ds(0, DEEP)],
        send_sem=fwd_send,
        recv_sem=fwd_recv,
        device_id=sibling,
        device_id_type=MESH,
    )
    forwarded.wait_recv()
    pl.semaphore_wait(ready, 3)
    for p in range(KC):
        label = beta[p]
        both = jnp.concatenate([abuf[label], abuf[partner[label]]], axis=0)
        sym = jnp.dot(order, both, preferred_element_type=F32).astype(BF16)
        symbuf[0, p] = sym[:HALF]
        symbuf[1, p] = sym[HALF:]
    def send_rows(h):
        lhs[h, pos] = symbuf[h, kc]

        @pl.loop(1, POS)
        def _(step):
            to = (pos + step) % POS
            pltpu.make_async_remote_copy(
                src_ref=symbuf.at[h, to // OCC],
                dst_ref=lhs.at[h, pos],
                send_sem=h2_send.at[h],
                recv_sem=h2_recv.at[h],
                device_id=place(to, kb),
                device_id_type=MESH,
            ).start()

    def lhs_wait(h):
        return pltpu.make_async_remote_copy(
            src_ref=lhs.at[h, pl.ds(0, POS - 1)],
            dst_ref=lhs.at[h, pl.ds(0, POS - 1)],
            send_sem=h2_send.at[h],
            recv_sem=h2_recv.at[h],
            device_id=sibling,
            device_id_type=MESH,
        )

    def multiply(h, first, last):
        left = jnp.concatenate(
            [
                lhs[h, 0:GROUPS].reshape(ROWS, LANES),
                lhs[h, GROUPS:POS].reshape(ROWS, LANES),
            ],
            axis=1,
        )

        @pl.loop(first, last)
        def _(step):
            sub = step // (TILES // CHUNK)
            chunk = step % (TILES // CHUNK)
            at = pl.multiple_of(chunk * (CHUNK * 2 * LANES), CHUNK * 2 * LANES)
            down = pl.multiple_of((3 - sub) * DEPTH, DEPTH)
            weight = jnp.concatenate(
                [
                    ztop[pl.ds(down, 4 * DEPTH), pl.ds(at, CHUNK * 2 * LANES)],
                    zbot[pl.ds(down, 4 * DEPTH), pl.ds(at, CHUNK * 2 * LANES)],
                ],
                axis=0,
            )
            product = jnp.dot(left, weight, preferred_element_type=F32)
            den_row = row_den[h, sub]
            parts = []
            for s in range(CHUNK):
                den = den_row + col_den[chunk * CHUNK + s, 0:1, :]
                inverse = jnp.clip(pltpu.reciprocal(den, approx=True), -1.0, 1.0)
                lo = s * 2 * LANES
                parts.append((product[:, lo : lo + LANES] * inverse).astype(BF16))
                parts.append((product[:, lo + LANES : lo + 2 * LANES] * inverse).astype(BF16))
            scaled = jnp.concatenate(parts, axis=1)
            acc[...] += lax.dot_general(
                scaled, weight, (((1,), (1,)), ((), ())), preferred_element_type=F32
            )

    def send_partials(h):
        packed = jnp.dot(perm, acc[...].astype(BF16), preferred_element_type=F32).astype(BF16)
        for r in range(POS):
            o1_send[h, r] = packed[r * 16 : (r + 1) * 16]
        o1_recv[h][pos] = o1_send[h, pos]

        @pl.loop(1, POS)
        def _(step):
            to = (pos + step) % POS
            pltpu.make_async_remote_copy(
                src_ref=o1_send.at[h, to],
                dst_ref=o1_recv[h].at[pos],
                send_sem=p1_send.at[h],
                recv_sem=p1_recv.at[h],
                device_id=place(to, kb),
                device_id_type=MESH,
            ).start()

    def partials_wait(h):
        return pltpu.make_async_remote_copy(
            src_ref=o1_send.at[h, pl.ds(0, POS - 1)],
            dst_ref=o1_recv[h].at[pl.ds(0, POS - 1)],
            send_sem=p1_send.at[h],
            recv_sem=p1_recv.at[h],
            device_id=sibling,
            device_id_type=MESH,
        )

    def core_copy(h):
        return pltpu.make_async_remote_copy(
            src_ref=sums.at[h, 1 - core],
            dst_ref=sums_recv.at[h],
            send_sem=sib_send.at[h],
            recv_sem=sib_recv.at[h],
            device_id=sibling,
            device_id_type=MESH,
        )

    def sum_plane(h):
        partials_wait(h).wait_recv()
        for label in range(KB):
            p = holder[label]
            total = o1_recv[h][p * OCC].astype(F32) + o1_recv[h][p * OCC + 1].astype(F32)
            sums[h, 0, label] = total[:, :LANES]
            sums[h, 1, label] = total[:, LANES:]
        core_copy(h).start()

    def send_sums(h):
        core_copy(h).wait_recv()
        o2_send[h] = (sums[h, core] + sums_recv[h]).astype(BF16)
        o2_recv[h, z] = o2_send[h, pl.ds(2 * z, 2)]
        for step in ORDER:
            pltpu.make_async_remote_copy(
                src_ref=o2_send.at[h, pl.ds((z + step) % DEEP * 2, 2)],
                dst_ref=o2_recv.at[h, z],
                send_sem=p2_send.at[h],
                recv_sem=p2_recv.at[h],
                device_id=along_z(step),
                device_id_type=MESH,
            ).start()

    def sums_wait(h):
        return pltpu.make_async_remote_copy(
            src_ref=o2_recv.at[h, pl.ds(0, DEEP - 1)],
            dst_ref=o2_recv.at[h, pl.ds(0, DEEP - 1)],
            send_sem=p2_send.at[h],
            recv_sem=p2_recv.at[h],
            device_id=sibling,
            device_id_type=MESH,
        )

    def last_copy(h):
        return pltpu.make_async_remote_copy(
            src_ref=last_send.at[h, 1 - core],
            dst_ref=last_recv.at[h],
            send_sem=last_sems.at[h],
            recv_sem=last_sems.at[2 + h],
            device_id=sibling,
            device_id_type=MESH,
        )

    def send_last(h):
        sums_wait(h).wait_recv()
        for c in range(2):
            total = o2_recv[h, 0, c].astype(F32)
            for deep in range(1, DEEP):
                total = total + o2_recv[h, deep, c].astype(F32)
            last_send[h, c] = total
        last_copy(h).start()

    def finish(h):
        last_copy(h).wait_recv()
        for at, total in ((core, last_send[h, core]), (1 - core, last_recv[h])):
            for g in range(GROUPS):
                out[0, at, 2 * h : 2 * h + 2, g * LANES : (g + 1) * LANES] = total[2 * g : 2 * g + 2]

    steps = 4 * TILES // CHUNK
    send_rows(0)
    lhs_wait(0).wait_recv()
    send_rows(1)
    acc[...] = jnp.zeros_like(acc)
    multiply(0, 0, steps)
    send_partials(0)
    lhs_wait(1).wait_recv()
    acc[...] = jnp.zeros_like(acc)
    multiply(1, 0, steps // 2)
    sum_plane(0)
    multiply(1, steps // 2, 3 * steps // 4)
    send_sums(0)
    multiply(1, 3 * steps // 4, steps)
    send_partials(1)
    send_last(0)
    sum_plane(1)
    finish(0)
    send_sums(1)
    pltpu.make_async_remote_copy(
        src_ref=abuf.at[pl.ds(0, DEEP - 1)],
        dst_ref=abuf.at[pl.ds(0, DEEP - 1)],
        send_sem=h1_send,
        recv_sem=fwd_recv,
        device_id=sibling,
        device_id_type=MESH,
    ).wait_send()
    forwarded.wait_send()
    for h in range(2):
        lhs_wait(h).wait_send()
        partials_wait(h).wait_send()
        core_copy(h).wait_send()
    send_last(1)
    finish(1)
    for h in range(2):
        sums_wait(h).wait_send()
        last_copy(h).wait_send()


def shards(amplitudes, integrals, eps_occ, eps_vir, conserve, partner):
    return pl.pallas_call(
        kernel,
        out_shape=jax.ShapeDtypeStruct((1, 2, 4, GROUPS * LANES), F32),
        in_specs=[pl.BlockSpec(memory_space=pl.ANY)] * 6,
        out_specs=pl.BlockSpec(memory_space=pltpu.VMEM),
        scratch_shapes=[
            pltpu.SMEM((KB, KB), jnp.int32),
            pltpu.SMEM((KB,), jnp.int32),
            pltpu.SMEM((8,), F32),
            pltpu.SMEM((KB, DEPTH), F32),
            pltpu.VMEM((1, 2, DEPTH, 4, 1024), BF16),
            pltpu.SemaphoreType.DMA((5,)),
            pltpu.VMEM((KB, PAIRS, LANES), BF16),
            pltpu.VMEM((2, KC, HALF, LANES), BF16),
            pltpu.VMEM((2, POS, HALF, LANES), BF16),
            pltpu.VMEM((7 * DEPTH, TILES * 2 * LANES), BF16),
            pltpu.VMEM((7 * DEPTH, TILES * 2 * LANES), BF16),
            pltpu.VMEM((2, 4, ROWS, LANES), F32),
            pltpu.VMEM((TILES, 8, LANES), F32),
            pltpu.VMEM((ROWS, 2 * LANES), F32),
            pltpu.VMEM((2, POS, 16, 2 * LANES), BF16),
            pltpu.VMEM((POS + OCC, 16, 2 * LANES), BF16),
            pltpu.VMEM((POS + OCC, 16, 2 * LANES), BF16),
            pltpu.VMEM((2, 2, KB, 16, LANES), F32),
            pltpu.VMEM((2, KB, 16, LANES), F32),
            pltpu.VMEM((2, KB, 16, LANES), BF16),
            pltpu.VMEM((2, DEEP, 2, 16, LANES), BF16),
            pltpu.VMEM((2, 2, 16, LANES), F32),
            pltpu.VMEM((2, 16, LANES), F32),
            pltpu.SMEM((KC,), jnp.int32),
            pltpu.SMEM((KB,), jnp.int32),
            pltpu.SemaphoreType.REGULAR,
            pltpu.SemaphoreType.DMA,
            pltpu.SemaphoreType.DMA,
            pltpu.SemaphoreType.DMA((DEEP,)),
            pltpu.SemaphoreType.DMA,
            pltpu.SemaphoreType.DMA,
        ]
        + [pltpu.SemaphoreType.DMA((2,))] * 8
        + [pltpu.SemaphoreType.DMA((4,))],
        compiler_params=pltpu.CompilerParams(
            collective_id=0, has_side_effects=True, vmem_limit_bytes=60 * 2**20
        ),
        name="lambda_source",
    )(conserve, partner, eps_occ, eps_vir, amplitudes, integrals)


def solution(mesh):
    in_specs = (P("kb", None, None, None), P("kb", None, None, "occ", None), P(), P(), P(), P())
    out_specs = P("kb", None, ("kc", "occ"), None)
    return jax.shard_map(shards, mesh=mesh, in_specs=in_specs, out_specs=out_specs, check_vma=False)
```

time: 62.2 us -> 57.5 us (0.924)
  Pallas kernels: 60.6 us -> 55.9 us
    pallas_call x1, Pallas kernels: 60.6 us -> 55.9 us  [shards(): pl.pallas_call(kernel, out_shape=jax.ShapeDtypeStruct((1, 2, 4, GROUPS *...]
    unnamed x0 -> x1, local copies, waits for them, and re-layouts: none -> 1.38 us
    transpose x1 -> x0, local copies, waits for them, and re-layouts: 0.76 us -> none  [shards(): jnp.transpose(result, (1, 0, 3, 2, 4)).reshape(1, 2, 4, GROUPS * LANES)]
    reshape x1 -> x0, local copies, waits for them, and re-layouts: 0.63 us -> none  [shards(): jnp.transpose(result, (1, 0, 3, 2, 4)).reshape(1, 2, 4, GROUPS * LANES)]
where the time goes in v1:
time: 57.5 us; the launch traced here: 57.3 us
  Pallas kernels  55.9 us (97%)
  local copies, waits for them, and re-layouts  1.38 us (2%)
    pallas_call x1, Pallas kernels, shards(): pl.pallas_call(kernel, out_shape=jax.ShapeDtypeStruct((1, 2, 4, GROUPS *...  55.9 us
    unnamed x1, local copies, waits for them, and re-layouts  1.38 us

profile of v1, /device:TPU:1, one launch (start us, length us, event | category | flops | bytes accessed | tf_op | source)
XLA Modules:
  0.0 57.3 jit_solution(1642468570389331509)
XLA Ops:
  0.0 55.9 %lambda_source.1 = f32[1,2,4,1024]{3,2,1,0:T(4,128)} custom-call(s32[16,16]{1,0:T(8,128)} %conserve_in.1, s32[16]{0:T(128)} %partner_in.1, f32[8]{0:T(128)} %eps_occ_in.1, f32[16,32]{1,0:T(8,128)} %eps_vir_in.1, bf16[1,2,64,1024]{3,2,1,0:T(8,128)(2,1)} %amp.1, bf16[1,2,32,4,1024]{4,3,2,1,0:T(4,128)(2,1)} %slab_in.1), custom_call_target="tpu_custom_call" | custom-call | tf_op jit(solution)/shard_map/lambda_source/pallas_call | solution.py:421
  55.9 1.4 %copy.8 = f32[1,2,4,1024]{3,2,1,0:T(4,128)} copy(f32[1,2,4,1024]{3,2,1,0:T(4,128)} %lambda_source.1) | data formatting | bytes 65536

commit v2 on v1

--- a/solution.py
+++ b/solution.py
@@ -20,6 +20,7 @@
 TILES = 32
 CHUNK = 32
 SHIFT = 2.0**-18
+WIDTHS = (2 * LANES, LANES, LANES)
 DEEP = 8
 ORDER = (1, 7, 2, 6, 3, 5, 4)
 MESH = pl.DeviceIdType.MESH
@@ -33,9 +34,10 @@
 
 def kernel(
     conserve_in, partner_in, eps_occ_in, eps_vir_in, amp, slab_in, out,
-    conserve, partner, eps_occ, eps_vir, slab, load_sem, abuf, symbuf, lhs, ztop, zbot, row_den, col_den, acc, o1_send, o1_recv0, o1_recv1,
-    sums, sums_recv, o2_send, o2_recv, last_send, last_recv, beta, holder, ready, copy_sem, h1_send, h1_recv, fwd_send, fwd_recv,
-    h2_send, h2_recv, p1_send, p1_recv, sib_send, sib_recv, p2_send, p2_recv, last_sems,
+    conserve, partner, eps_occ, eps_vir, slab, load_sem, abuf, symbuf, lhs, ztop, zbot, row_den, col_den, acc0, acc1,
+    o1_send0, o1_send1, o1_send2, o1_recv0, o1_recv1, o1_recv2,
+    o2_send0, o2_send1, o2_send2, o2_recv0, o2_recv1, o2_recv2, beta, holder, ready, copy_sem,
+    h1_send, h1_recv, fwd_send, fwd_recv, h2_send, h2_recv, p1_send, p1_recv, p2_send, p2_recv,
 ):
     kc = lax.axis_index("kc")
     kb = lax.axis_index("kb")
@@ -57,9 +59,19 @@
         to = (y + step) % 4
         return {"kc": x * 2 + to % 2, "occ": to // 2}
 
-    o1_recv = (o1_recv0, o1_recv1)
+    acc = (acc0, acc1, acc1)
+    o1_send = (o1_send0, o1_send1, o1_send2)
+    o1_recv = (o1_recv0, o1_recv1, o1_recv2)
+    o2_send = (o2_send0, o2_send1, o2_send2)
+    o2_recv = (o2_recv0, o2_recv1, o2_recv2)
     barrier = pltpu.get_barrier_semaphore()
 
+    own = pltpu.make_async_copy(
+        amp.at[0, part, :, pl.ds(pl.multiple_of(group * LANES, LANES), LANES)],
+        abuf.at[kb],
+        copy_sem,
+    )
+    own.start()
     for step in ORDER:
         pl.semaphore_signal(barrier, inc=1, device_id=along_z(step), device_id_type=MESH)
     pl.semaphore_signal(barrier, inc=1, device_id=sibling, device_id_type=MESH)
@@ -72,12 +84,6 @@
         )
         pl.semaphore_signal(barrier, inc=1, device_id=along_y(step), device_id_type=MESH)
 
-    own = pltpu.make_async_copy(
-        amp.at[0, part, :, pl.ds(pl.multiple_of(group * LANES, LANES), LANES)],
-        abuf.at[kb],
-        copy_sem,
-    )
-    own.start()
     loads = [
         pltpu.make_async_copy(source, target, load_sem.at[at])
         for at, (source, target) in enumerate(
@@ -174,9 +180,9 @@
         for k in range(4):
             col_den[k * 8 + u] = eps_occ[occ * 4 + k] - vir_bc
 
-    for zero in range(OCC):
-        o1_recv0[POS + zero] = jnp.zeros((16, 2 * LANES), BF16)
-        o1_recv1[POS + zero] = jnp.zeros((16, 2 * LANES), BF16)
+    for landing in o1_recv:
+        for zero in range(OCC):
+            landing[POS + zero] = jnp.zeros(landing.shape[1:], BF16)
 
     out_row = lax.broadcasted_iota(jnp.int32, (PAIRS, 2 * PAIRS), 0)
     in_col = lax.broadcasted_iota(jnp.int32, (PAIRS, 2 * PAIRS), 1)
@@ -246,7 +252,8 @@
             device_id_type=MESH,
         )
 
-    def multiply(h, first, last):
+    def multiply(unit, h, first, last):
+        acc[unit][...] = jnp.zeros_like(acc[unit])
         left = jnp.concatenate(
             [
                 lhs[h, 0:GROUPS].reshape(ROWS, LANES),
@@ -278,125 +285,111 @@
                 parts.append((product[:, lo : lo + LANES] * inverse).astype(BF16))
                 parts.append((product[:, lo + LANES : lo + 2 * LANES] * inverse).astype(BF16))
             scaled = jnp.concatenate(parts, axis=1)
-            acc[...] += lax.dot_general(
-                scaled, weight, (((1,), (1,)), ((), ())), preferred_element_type=F32
+            if unit == 0:
+                back = weight
+            else:
+                near = pl.multiple_of((3 - sub % 2) * DEPTH, DEPTH)
+                back = jnp.concatenate(
+                    [
+                        ztop[pl.ds(near, 2 * DEPTH), pl.ds(at, CHUNK * 2 * LANES)],
+                        zbot[pl.ds(near, 2 * DEPTH), pl.ds(at, CHUNK * 2 * LANES)],
+                    ],
+                    axis=0,
+                )
+            acc[unit][...] += lax.dot_general(
+                scaled, back, (((1,), (1,)), ((), ())), preferred_element_type=F32
             )
 
-    def send_partials(h):
-        packed = jnp.dot(perm, acc[...].astype(BF16), preferred_element_type=F32).astype(BF16)
+    def send_partials(unit):
+        sums = acc[unit][...].astype(BF16)
+        packed = jnp.dot(perm, sums, preferred_element_type=F32).astype(BF16)
         for r in range(POS):
-            o1_send[h, r] = packed[r * 16 : (r + 1) * 16]
-        o1_recv[h][pos] = o1_send[h, pos]
+            o1_send[unit][r] = packed[r * 16 : (r + 1) * 16]
+        o1_recv[unit][pos] = o1_send[unit][pos]
 
         @pl.loop(1, POS)
         def _(step):
             to = (pos + step) % POS
             pltpu.make_async_remote_copy(
-                src_ref=o1_send.at[h, to],
-                dst_ref=o1_recv[h].at[pos],
-                send_sem=p1_send.at[h],
-                recv_sem=p1_recv.at[h],
+                src_ref=o1_send[unit].at[to],
+                dst_ref=o1_recv[unit].at[pos],
+                send_sem=p1_send.at[unit],
+                recv_sem=p1_recv.at[unit],
                 device_id=place(to, kb),
                 device_id_type=MESH,
             ).start()
 
-    def partials_wait(h):
+    def partials_wait(unit):
         return pltpu.make_async_remote_copy(
-            src_ref=o1_send.at[h, pl.ds(0, POS - 1)],
-            dst_ref=o1_recv[h].at[pl.ds(0, POS - 1)],
-            send_sem=p1_send.at[h],
-            recv_sem=p1_recv.at[h],
+            src_ref=o1_send[unit].at[pl.ds(0, POS - 1)],
+            dst_ref=o1_recv[unit].at[pl.ds(0, POS - 1)],
+            send_sem=p1_send.at[unit],
+            recv_sem=p1_recv.at[unit],
             device_id=sibling,
             device_id_type=MESH,
         )
 
-    def core_copy(h):
-        return pltpu.make_async_remote_copy(
-            src_ref=sums.at[h, 1 - core],
-            dst_ref=sums_recv.at[h],
-            send_sem=sib_send.at[h],
-            recv_sem=sib_recv.at[h],
-            device_id=sibling,
-            device_id_type=MESH,
-        )
-
-    def sum_plane(h):
-        partials_wait(h).wait_recv()
+    def send_sums(unit):
+        partials_wait(unit).wait_recv()
         for label in range(KB):
-            p = holder[label]
-            total = o1_recv[h][p * OCC].astype(F32) + o1_recv[h][p * OCC + 1].astype(F32)
-            sums[h, 0, label] = total[:, :LANES]
-            sums[h, 1, label] = total[:, LANES:]
-        core_copy(h).start()
-
-    def send_sums(h):
-        core_copy(h).wait_recv()
-        o2_send[h] = (sums[h, core] + sums_recv[h]).astype(BF16)
-        o2_recv[h, z] = o2_send[h, pl.ds(2 * z, 2)]
-        for step in ORDER:
+            at = holder[label] * OCC
+            total = o1_recv[unit][at].astype(F32) + o1_recv[unit][at + 1].astype(F32)
+            o2_send[unit][label] = total.astype(BF16)
+        o2_recv[unit][kb] = o2_send[unit][kb]
+
+        @pl.loop(1, KB)
+        def _(step):
+            to = (kb + step) % KB
             pltpu.make_async_remote_copy(
-                src_ref=o2_send.at[h, pl.ds((z + step) % DEEP * 2, 2)],
-                dst_ref=o2_recv.at[h, z],
-                send_sem=p2_send.at[h],
-                recv_sem=p2_recv.at[h],
-                device_id=along_z(step),
+                src_ref=o2_send[unit].at[to],
+                dst_ref=o2_recv[unit].at[kb],
+                send_sem=p2_send.at[unit],
+                recv_sem=p2_recv.at[unit],
+                device_id={"kb": to},
                 device_id_type=MESH,
             ).start()
 
-    def sums_wait(h):
+    def sums_wait(unit):
         return pltpu.make_async_remote_copy(
-            src_ref=o2_recv.at[h, pl.ds(0, DEEP - 1)],
-            dst_ref=o2_recv.at[h, pl.ds(0, DEEP - 1)],
-            send_sem=p2_send.at[h],
-            recv_sem=p2_recv.at[h],
+            src_ref=o2_send[unit].at[pl.ds(0, KB - 1)],
+            dst_ref=o2_recv[unit].at[pl.ds(0, KB - 1)],
+            send_sem=p2_send.at[unit],
+            recv_sem=p2_recv.at[unit],
             device_id=sibling,
             device_id_type=MESH,
         )
 
-    def last_copy(h):
-        return pltpu.make_async_remote_copy(
-            src_ref=last_send.at[h, 1 - core],
-            dst_ref=last_recv.at[h],
-            send_sem=last_sems.at[h],
-            recv_sem=last_sems.at[2 + h],
-            device_id=sibling,
-            device_id_type=MESH,
-        )
-
-    def send_last(h):
-        sums_wait(h).wait_recv()
+    def total_of(unit):
+        sums_wait(unit).wait_recv()
+        total = o2_recv[unit][0].astype(F32)
+        for label in range(1, KB):
+            total = total + o2_recv[unit][label].astype(F32)
+        return total
+
+    def finish(h, parts):
         for c in range(2):
-            total = o2_recv[h, 0, c].astype(F32)
-            for deep in range(1, DEEP):
-                total = total + o2_recv[h, deep, c].astype(F32)
-            last_send[h, c] = total
-        last_copy(h).start()
-
-    def finish(h):
-        last_copy(h).wait_recv()
-        for at, total in ((core, last_send[h, core]), (1 - core, last_recv[h])):
             for g in range(GROUPS):
-                out[0, at, 2 * h : 2 * h + 2, g * LANES : (g + 1) * LANES] = total[2 * g : 2 * g + 2]
+                out[0, c, 2 * h : 2 * h + 2, g * LANES : (g + 1) * LANES] = parts[c][
+                    2 * g : 2 * g + 2
+                ]
 
     steps = 4 * TILES // CHUNK
+    half = steps // 2
     send_rows(0)
     lhs_wait(0).wait_recv()
     send_rows(1)
-    acc[...] = jnp.zeros_like(acc)
-    multiply(0, 0, steps)
+    multiply(0, 0, 0, steps)
     send_partials(0)
     lhs_wait(1).wait_recv()
-    acc[...] = jnp.zeros_like(acc)
-    multiply(1, 0, steps // 2)
-    sum_plane(0)
-    multiply(1, steps // 2, 3 * steps // 4)
+    multiply(1, 1, 0, half)
+    send_partials(1)
     send_sums(0)
-    multiply(1, 3 * steps // 4, steps)
-    send_partials(1)
-    send_last(0)
-    sum_plane(1)
-    finish(0)
+    multiply(2, 1, half, steps)
+    send_partials(2)
     send_sums(1)
+    whole = total_of(0)
+    finish(0, (whole[:, :LANES], whole[:, LANES:]))
+    send_sums(2)
     pltpu.make_async_remote_copy(
         src_ref=abuf.at[pl.ds(0, DEEP - 1)],
         dst_ref=abuf.at[pl.ds(0, DEEP - 1)],
@@ -408,13 +401,20 @@
     forwarded.wait_send()
     for h in range(2):
         lhs_wait(h).wait_send()
-        partials_wait(h).wait_send()
-        core_copy(h).wait_send()
-    send_last(1)
-    finish(1)
-    for h in range(2):
-        sums_wait(h).wait_send()
-        last_copy(h).wait_send()
+    for unit in range(3):
+        partials_wait(unit).wait_send()
+    lane = lax.broadcasted_iota(jnp.int32, (16, LANES), 1)
+    first = total_of(1)
+    second = total_of(2)
+    finish(
+        1,
+        (
+            jnp.where(lane < 64, first, pltpu.roll(second, 64, 1)),
+            jnp.where(lane < 64, pltpu.roll(first, 64, 1), second),
+        ),
+    )
+    for unit in range(3):
+        sums_wait(unit).wait_send()
 
 
 def shards(amplitudes, integrals, eps_occ, eps_vir, conserve, partner):
@@ -438,15 +438,12 @@
             pltpu.VMEM((2, 4, ROWS, LANES), F32),
             pltpu.VMEM((TILES, 8, LANES), F32),
             pltpu.VMEM((ROWS, 2 * LANES), F32),
-            pltpu.VMEM((2, POS, 16, 2 * LANES), BF16),
-            pltpu.VMEM((POS + OCC, 16, 2 * LANES), BF16),
-            pltpu.VMEM((POS + OCC, 16, 2 * LANES), BF16),
-            pltpu.VMEM((2, 2, KB, 16, LANES), F32),
-            pltpu.VMEM((2, KB, 16, LANES), F32),
-            pltpu.VMEM((2, KB, 16, LANES), BF16),
-            pltpu.VMEM((2, DEEP, 2, 16, LANES), BF16),
-            pltpu.VMEM((2, 2, 16, LANES), F32),
-            pltpu.VMEM((2, 16, LANES), F32),
+            pltpu.VMEM((ROWS, LANES), F32),
+        ]
+        + [pltpu.VMEM((POS, 16, width), BF16) for width in WIDTHS]
+        + [pltpu.VMEM((POS + OCC, 16, width), BF16) for width in WIDTHS]
+        + [pltpu.VMEM((KB, 16, width), BF16) for width in WIDTHS] * 2
+        + [
             pltpu.SMEM((KC,), jnp.int32),
             pltpu.SMEM((KB,), jnp.int32),
             pltpu.SemaphoreType.REGULAR,
@@ -456,8 +453,8 @@
             pltpu.SemaphoreType.DMA,
             pltpu.SemaphoreType.DMA,
         ]
-        + [pltpu.SemaphoreType.DMA((2,))] * 8
-        + [pltpu.SemaphoreType.DMA((4,))],
+        + [pltpu.SemaphoreType.DMA((2,))] * 2
+        + [pltpu.SemaphoreType.DMA((3,))] * 4,
         compiler_params=pltpu.CompilerParams(
             collective_id=0, has_side_effects=True, vmem_limit_bytes=60 * 2**20
         ),

time: 57.5 us -> 55.6 us (0.967)
  Pallas kernels: 55.9 us -> 54.1 us
    pallas_call x1, Pallas kernels: 55.9 us -> 54.1 us  [shards(): pl.pallas_call(kernel, out_shape=jax.ShapeDtypeStruct((1, 2, 4, GROUPS *...]
where the time goes in v2:
time: 55.6 us; the launch traced here: 55.5 us
  Pallas kernels  54.1 us (97%)
  local copies, waits for them, and re-layouts  1.38 us (2%)
    pallas_call x1, Pallas kernels, shards(): pl.pallas_call(kernel, out_shape=jax.ShapeDtypeStruct((1, 2, 4, GROUPS *...  54.1 us
    unnamed x1, local copies, waits for them, and re-layouts  1.38 us

profile of v2, /device:TPU:1, one launch (start us, length us, event | category | flops | bytes accessed | tf_op | source)
XLA Modules:
  0.0 55.5 jit_solution(7798633929810646112)
XLA Ops:
  0.0 54.1 %lambda_source.1 = f32[1,2,4,1024]{3,2,1,0:T(4,128)} custom-call(s32[16,16]{1,0:T(8,128)} %conserve_in.1, s32[16]{0:T(128)} %partner_in.1, f32[8]{0:T(128)} %eps_occ_in.1, f32[16,32]{1,0:T(8,128)} %eps_vir_in.1, bf16[1,2,64,1024]{3,2,1,0:T(8,128)(2,1)} %amp.1, bf16[1,2,32,4,1024]{4,3,2,1,0:T(4,128)(2,1)} %slab_in.1), custom_call_target="tpu_custom_call" | custom-call | tf_op jit(solution)/shard_map/lambda_source/pallas_call | solution.py:421
  54.1 1.4 %copy.8 = f32[1,2,4,1024]{3,2,1,0:T(4,128)} copy(f32[1,2,4,1024]{3,2,1,0:T(4,128)} %lambda_source.1) | data formatting | bytes 65536

commit v3 on v2

--- a/solution.py
+++ b/solution.py
@@ -262,7 +262,7 @@
             axis=1,
         )
 
-        @pl.loop(first, last)
+        @pl.loop(first, last, unroll=2 if unit == 0 else 1)
         def _(step):
             sub = step // (TILES // CHUNK)
             chunk = step % (TILES // CHUNK)

time: 55.6 us -> 55.2 us (level)
  no operation moved by 1% of the time
where the time goes in v3:
time: 55.2 us; the launch traced here: 55.1 us
  Pallas kernels  53.7 us (97%)
  local copies, waits for them, and re-layouts  1.38 us (2%)
    pallas_call x1, Pallas kernels, shards(): pl.pallas_call(kernel, out_shape=jax.ShapeDtypeStruct((1, 2, 4, GROUPS *...  53.7 us
    unnamed x1, local copies, waits for them, and re-layouts  1.38 us

profile of v3, /device:TPU:1, one launch (start us, length us, event | category | flops | bytes accessed | tf_op | source)
XLA Modules:
  0.0 55.1 jit_solution(9937157942970461926)
XLA Ops:
  0.0 53.7 %lambda_source.1 = f32[1,2,4,1024]{3,2,1,0:T(4,128)} custom-call(s32[16,16]{1,0:T(8,128)} %conserve_in.1, s32[16]{0:T(128)} %partner_in.1, f32[8]{0:T(128)} %eps_occ_in.1, f32[16,32]{1,0:T(8,128)} %eps_vir_in.1, bf16[1,2,64,1024]{3,2,1,0:T(8,128)(2,1)} %amp.1, bf16[1,2,32,4,1024]{4,3,2,1,0:T(4,128)(2,1)} %slab_in.1), custom_call_target="tpu_custom_call" | custom-call | tf_op jit(solution)/shard_map/lambda_source/pallas_call | solution.py:421
  53.7 1.4 %copy.8 = f32[1,2,4,1024]{3,2,1,0:T(4,128)} copy(f32[1,2,4,1024]{3,2,1,0:T(4,128)} %lambda_source.1) | data formatting | bytes 65536

commit v4 on v3

--- a/solution.py
+++ b/solution.py
@@ -387,9 +387,9 @@
     multiply(2, 1, half, steps)
     send_partials(2)
     send_sums(1)
+    send_sums(2)
     whole = total_of(0)
     finish(0, (whole[:, :LANES], whole[:, LANES:]))
-    send_sums(2)
     pltpu.make_async_remote_copy(
         src_ref=abuf.at[pl.ds(0, DEEP - 1)],
         dst_ref=abuf.at[pl.ds(0, DEEP - 1)],

time: 55.2 us -> 55.2 us (level)
  no operation moved by 1% of the time
where the time goes in v4:
time: 55.2 us; the launch traced here: 55.1 us
  Pallas kernels  53.7 us (97%)
  local copies, waits for them, and re-layouts  1.38 us (2%)
    pallas_call x1, Pallas kernels, shards(): pl.pallas_call(kernel, out_shape=jax.ShapeDtypeStruct((1, 2, 4, GROUPS *...  53.7 us
    unnamed x1, local copies, waits for them, and re-layouts  1.38 us

profile of v4, /device:TPU:1, one launch (start us, length us, event | category | flops | bytes accessed | tf_op | source)
XLA Modules:
  0.0 55.1 jit_solution(12986584619745368541)
XLA Ops:
  0.0 53.7 %lambda_source.1 = f32[1,2,4,1024]{3,2,1,0:T(4,128)} custom-call(s32[16,16]{1,0:T(8,128)} %conserve_in.1, s32[16]{0:T(128)} %partner_in.1, f32[8]{0:T(128)} %eps_occ_in.1, f32[16,32]{1,0:T(8,128)} %eps_vir_in.1, bf16[1,2,64,1024]{3,2,1,0:T(8,128)(2,1)} %amp.1, bf16[1,2,32,4,1024]{4,3,2,1,0:T(4,128)(2,1)} %slab_in.1), custom_call_target="tpu_custom_call" | custom-call | tf_op jit(solution)/shard_map/lambda_source/pallas_call | solution.py:421
  53.7 1.4 %copy.8 = f32[1,2,4,1024]{3,2,1,0:T(4,128)} copy(f32[1,2,4,1024]{3,2,1,0:T(4,128)} %lambda_source.1) | data formatting | bytes 65536

commit v5 on v3

--- a/solution.py
+++ b/solution.py
@@ -262,7 +262,7 @@
             axis=1,
         )
 
-        @pl.loop(first, last, unroll=2 if unit == 0 else 1)
+        @pl.loop(first, last, unroll=2 if unit < 2 else 1)
         def _(step):
             sub = step // (TILES // CHUNK)
             chunk = step % (TILES // CHUNK)

time: 55.2 us -> 55.3 us (level)
  no operation moved by 1% of the time
where the time goes in v5:
time: 55.3 us; the launch traced here: 55.2 us
  Pallas kernels  53.8 us (97%)
  local copies, waits for them, and re-layouts  1.38 us (2%)
    pallas_call x1, Pallas kernels, shards(): pl.pallas_call(kernel, out_shape=jax.ShapeDtypeStruct((1, 2, 4, GROUPS *...  53.8 us
    unnamed x1, local copies, waits for them, and re-layouts  1.38 us

profile of v5, /device:TPU:1, one launch (start us, length us, event | category | flops | bytes accessed | tf_op | source)
XLA Modules:
  0.0 55.2 jit_solution(18139745408341842282)
XLA Ops:
  0.0 53.8 %lambda_source.1 = f32[1,2,4,1024]{3,2,1,0:T(4,128)} custom-call(s32[16,16]{1,0:T(8,128)} %conserve_in.1, s32[16]{0:T(128)} %partner_in.1, f32[8]{0:T(128)} %eps_occ_in.1, f32[16,32]{1,0:T(8,128)} %eps_vir_in.1, bf16[1,2,64,1024]{3,2,1,0:T(8,128)(2,1)} %amp.1, bf16[1,2,32,4,1024]{4,3,2,1,0:T(4,128)(2,1)} %slab_in.1), custom_call_target="tpu_custom_call" | custom-call | tf_op jit(solution)/shard_map/lambda_source/pallas_call | solution.py:421
  53.8 1.4 %copy.8 = f32[1,2,4,1024]{3,2,1,0:T(4,128)} copy(f32[1,2,4,1024]{3,2,1,0:T(4,128)} %lambda_source.1) | data formatting | bytes 65536
